TPU v7x, 1024 devices: a whole 4x8x16 slice. The times are simulated.
1024 devices in a mesh: blk: 64 (over x_lo, z, core), group: 16 (over y, x_hi).
Axes of the slice: x: 4 (x_hi: 2, x_lo: 2; x = x_hi * 2 + x_lo), y: 8, z: 16, core: 2. Of those that a mesh axis runs over, the one named last changes fastest.
Arguments:
- patches: bfloat16 [385024, 1152], P(('blk', 'group')), may hold values from -6 to 6
- patch_counts: int32 [1024, 16], P(('blk', 'group')), may hold values from 1 to 31, as said below
- dest_list: int32 [1024, 16], P(('blk', 'group')), may hold values from 0 to 15, as said below
- probe: bfloat16 [1152], replicated, may hold values from -900 to 900
- w_attn_out: bfloat16 [1152, 1152], replicated, may hold values from -0.1875 to 0.1875
- w_key: bfloat16 [1152, 1152], replicated, may hold values from -0.1875 to 0.1875
- w_value: bfloat16 [1152, 1152], replicated, may hold values from -0.1875 to 0.1875
- texts: bfloat16 [16384, 1152], P(('blk', 'group')), may hold values from -6 to 6
- image_labels: int32 [16384], P(('blk', 'group')), may hold values from 0 to 255
- text_labels: int32 [16384], P(('blk', 'group')), may hold values from 0 to 255
- log_temp: float32 [1], replicated, may hold values from 4 to 4.8
- bias: float32 [1], replicated, may hold values from -4 to -2
Outputs:
- image_grad: bfloat16 [16384, 1152], P(('blk', 'group'))
- text_grad: bfloat16 [16384, 1152], P(('blk', 'group'))
- row_loss: float32 [16384], P(('blk', 'group'))
Inputs may be any that keep to these rules, and one draw needn't show every extreme that they name: `patch_counts`: one device's counts sum to at most 376, reached by a device of every block of 16 devices; the images that the devices of one such block send to one device (by dest_list) hold exactly 256 rows together. `dest_list`: each row names every device index of the group exactly once.
All inputs are finite; a program needn't handle non-finite values.
Results may differ from a plain program's by a relative error of at most 0.019.
Values may be sent and summed in bfloat16 or wider, within the bound.
A program may use at most 64 MiB of HBM per device.

v0:
```python
import functools

import jax
import jax.numpy as jnp
from jax import lax
from jax.experimental import pallas as pl
from jax.experimental.pallas import tpu as pltpu
from jax.sharding import PartitionSpec as P

HEADS = 16
LANES = 128
NEG = -1e30
F32 = jnp.float32
BF16 = jnp.bfloat16
NT = (((1,), (1,)), ((), ()))
TN = (((0,), (0,)), ((), ()))


def offsets(depth):
    if depth == 16:
        return ((0, 1, -1, 2), (-6, 6, -2, 2))
    if depth == 4:
        return ((0, 1), (-1, 1))
    raise ValueError("depth of z")


def parts(width):
    return 3 if width % (3 * LANES) == 0 else 1


def dot(a, b, dims=(((1,), (0,)), ((), ()))):
    return lax.dot_general(a, b, dims, preferred_element_type=F32)


def split(data, pieces):
    out = []
    for _ in range(pieces - 1):
        piece = data.astype(BF16)
        out.append(piece)
        data = data - piece.astype(F32)
    return out + [data.astype(BF16)]


def iota(shape, axis):
    return lax.broadcasted_iota(jnp.int32, shape, axis)


def column(row):
    n = row.shape[1]
    same = iota((n, n), 0) == iota((n, n), 1)
    return jnp.sum(jnp.where(same, jnp.broadcast_to(row, (n, n)), 0.0), axis=1, keepdims=True)


def unit(data):
    norm = jnp.sqrt(jnp.sum(data * data, axis=-1, keepdims=True) + 1e-06)
    return (data / norm, norm)


def back(grad, row_unit, norm):
    return (grad - row_unit * jnp.sum(row_unit * grad, axis=-1, keepdims=True)) / norm


def pool(patch, counts, dest, probe, key_w, proj_w, value_w, ready, normed):
    rows, width = patch.shape
    padded = normed.shape[0]
    head = width // HEADS
    images = counts.shape[1]
    cuts = parts(width)
    wide = width // cuts
    if padded > rows:
        normed[rows:padded, :] = jnp.zeros((padded - rows, width), F32)
    for cut in range(cuts):
        ready("proj", cut)
        normed[0:rows, cut * wide : (cut + 1) * wide] = dot(patch[...], proj_w[:, cut * wide : (cut + 1) * wide])
    proj = normed[0:rows, :]
    centre = proj - jnp.mean(proj, axis=-1, keepdims=True)
    normed[0:rows, :] = centre / jnp.sqrt(jnp.mean(centre * centre, axis=-1, keepdims=True) + 1e-06)
    low = iota((HEADS, width), 0) * head
    lane = iota((HEADS, width), 1)
    key_probe = []
    for cut in range(cuts):
        ready("key", cut)
        spread = jnp.where(
            (lane >= low) & (lane < low + head), jnp.broadcast_to(probe[...].astype(F32).reshape(1, width), (HEADS, width)), 0.0
        ).astype(BF16)
        key_probe.append(dot(spread, key_w[cut * wide : (cut + 1) * wide, :], NT))
    key_probe = jnp.concatenate(split(jnp.concatenate(key_probe, axis=1), 3), axis=0)
    pieces = split(normed[...], 2)
    scores = jnp.transpose(dot(pieces[1], key_probe, NT) + dot(pieces[0], key_probe, NT))
    scores = scores[:HEADS] + (scores[HEADS : 2 * HEADS] + scores[2 * HEADS : 3 * HEADS])
    scores = scores / jnp.sqrt(F32(head))
    image = iota((images, images), 0)
    which = iota((images, images), 1)
    lengths = jnp.broadcast_to(column(counts[...].astype(F32)), (images, images))
    first = jnp.sum(jnp.where(image < which, lengths, 0.0), axis=0, keepdims=True)
    last = jnp.sum(jnp.where(image <= which, lengths, 0.0), axis=0, keepdims=True)
    chosen = jnp.broadcast_to(dest[...], (images, images)) == image
    first = jnp.sum(jnp.where(chosen, jnp.broadcast_to(first, (images, images)), 0.0), axis=1, keepdims=True)
    last = jnp.sum(jnp.where(chosen, jnp.broadcast_to(last, (images, images)), 0.0), axis=1, keepdims=True)
    place = iota((images, padded), 1).astype(F32)
    member = ((place >= first) & (place < last))[None]
    masked = jnp.where(member, scores[:, None, :], NEG)
    expo = jnp.where(member, jnp.exp(masked - jnp.max(masked, axis=2, keepdims=True)), 0.0)
    weights = expo / jnp.sum(expo, axis=2, keepdims=True)
    weights = weights.reshape(HEADS * images, padded).astype(BF16)
    mixed = dot(weights, pieces[0]).astype(BF16)
    out = []
    for cut in range(cuts):
        ready("value", cut)
        first_head, last_head = cut * wide // head, -(-(cut + 1) * wide // head)
        taken = slice(first_head * images, last_head * images)
        full = dot(mixed[taken], value_w[:, cut * wide : (cut + 1) * wide])
        lane = iota((images, wide), 1) + cut * wide
        kept = jnp.zeros((images, wide), F32)
        for at in range(first_head, last_head):
            inside = (lane >= at * head) & (lane < at * head + head)
            kept = jnp.where(inside, full[(at - first_head) * images : (at - first_head + 1) * images], kept)
        out.append(kept)
    return jnp.concatenate(out, axis=1).astype(BF16).astype(F32)


def pairs(images, texts, width, temp, shift):
    logits = temp * dot(images[:, :width], texts[:, :width], NT) + shift
    apart = dot(images[:, width:], texts[:, width:], NT)
    signs = jnp.where(jnp.abs(apart) < 0.5, 1.0, -1.0).astype(F32)
    turned = -signs * logits
    small = jnp.exp(-jnp.abs(turned))
    loss = jnp.maximum(turned, 0.0) + jnp.log1p(small)
    sigmoid = jnp.where(turned >= 0, 1.0, small) / (1.0 + small)
    return (temp * -signs * sigmoid).astype(BF16), jnp.sum(loss, axis=1, keepdims=True)


def kernel(
    depth,
    peers,
    patches,
    counts_hbm,
    dest_hbm,
    probe_hbm,
    w_proj,
    w_key,
    w_value,
    texts,
    image_labels_hbm,
    text_labels_hbm,
    log_temp,
    bias,
    image_out,
    text_out,
    loss_out,
    counts,
    dest,
    probe,
    image_labels,
    text_labels,
    patch_buf,
    proj_buf,
    key_buf,
    value_buf,
    text_buf,
    normed,
    row_out,
    row_in,
    text_own,
    text_set,
    image_set,
    side_back,
    side_got,
    image_back,
    image_got,
    core_back,
    core_got,
    text_back,
    text_got,
    load_sem,
    row_send,
    row_recv,
    text_send,
    text_recv,
    image_send,
    image_recv,
    iback_send,
    iback_recv,
    tback_send,
    tback_recv,
    core_send,
    core_recv,
    side_send,
    side_recv,
):
    width = patches.shape[1]
    size = text_buf.shape[0]
    image_far, text_far = offsets(depth)
    reach = [(turn, far) for turn in (0, 1) for far in image_far]
    half = len(text_far) * size
    near = len(image_far)

    here = lax.axis_index("blk")
    mine = lax.axis_index("group")
    at_x, at_z, at_core = here // (2 * depth), (here // 2) % depth, here % 2
    way = 1 - 2 * at_core

    def blk(turn_x, far, turn_core):
        x = (at_x + turn_x) % 2
        z = (at_z + far + depth) % depth
        core = (at_core + turn_core) % 2
        return {"blk": (x * depth + z) * 2 + core}

    def remote(src, dst, send, recv, device):
        copy = pltpu.make_async_remote_copy(
            src_ref=src,
            dst_ref=dst,
            send_sem=send,
            recv_sem=recv,
            device_id=device,
            device_id_type=pl.DeviceIdType.MESH,
        )
        copy.start()
        return copy

    loads = {}

    def load(name, src, dst):
        loads[name] = pltpu.make_async_copy(src, dst, load_sem.at[len(loads)])
        loads[name].start()

    cuts = parts(width)
    wide = width // cuts
    load("patch", patches, patch_buf)
    for cut in range(cuts):
        some = pl.ds(cut * wide, wide)
        load(("proj", cut), w_proj.at[:, some], proj_buf.at[:, some])
    load("text", texts, text_buf)
    for name, src, dst in (
        ("counts", counts_hbm, counts),
        ("dest", dest_hbm, dest),
        ("probe", probe_hbm, probe),
        ("image_labels", image_labels_hbm, image_labels),
        ("text_labels", text_labels_hbm, text_labels),
    ):
        load(name, src, dst)
    for cut in range(cuts):
        some = pl.ds(cut * wide, wide)
        load(("key", cut), w_key.at[some, :], key_buf.at[some, :])
    for cut in range(cuts):
        some = pl.ds(cut * wide, wide)
        load(("value", cut), w_value.at[:, some], value_buf.at[:, some])

    known = {(turn, far % depth, 0) for turn, away in reach for far in (away, -away)}
    known |= {(0, far % depth, 0) for away in text_far for far in (away, -away)}
    known |= {(0, 0, 1)}
    known -= {(0, 0, 0)}
    barrier = pltpu.get_barrier_semaphore()
    for partner in sorted(known):
        pl.semaphore_signal(barrier, inc=1, device_id=blk(*partner), device_id_type=pl.DeviceIdType.MESH)
    for step in range(1, peers):
        pl.semaphore_signal(
            barrier, inc=1, device_id={"group": (mine + step) % peers}, device_id_type=pl.DeviceIdType.MESH
        )

    def block(ref, at, count=1):
        return ref.at[pl.ds(at * size, count * size), :]

    lane = iota((size, LANES), 1)
    loads["patch"].wait()
    text_copies = []
    kept = {}

    def ready(name, cut):
        loads[(name, cut)].wait()
        if name == "key" and cut == 0:
            for other in ("text", "counts", "dest", "probe", "image_labels", "text_labels"):
                loads[other].wait()
            text_unit, text_norm = unit(text_buf[...].astype(F32))
            kept["text"] = (text_unit, text_norm)
            text_own[:, 0:width] = text_unit.astype(BF16)
            text_label = column(text_labels[...].astype(F32))
            text_own[:, width:] = jnp.where(lane == 0, 1.0, jnp.where(lane == 1, -text_label, 0.0)).astype(BF16)

    ordered = pool(patch_buf, counts, dest, probe, key_buf, proj_buf, value_buf, ready, normed)
    for at in range(peers):
        row_out[at] = ordered[at : at + 1, :]
    pl.semaphore_wait(barrier, len(known) + peers - 1)
    row_copies = []
    for step in sorted(range(1, peers), key=lambda step: abs(step - peers // 2)):
        to = (mine + step) % peers
        row_copies.append(
            remote(
                row_out.at[to], row_in.at[mine], row_send.at[step], row_recv.at[step], {"group": to}
            )
        )
    row_in[mine] = row_out[mine]
    for at in range(len(text_far)):
        text_copies.append(
            remote(
                text_own,
                block(text_set, at),
                text_send.at[at],
                text_recv.at[at],
                blk(0, text_far[at], 0),
            )
        )

    for copy in row_copies:
        copy.wait_recv()
    placed = jnp.concatenate([row_in[at] for at in range(peers)], axis=0)
    image_unit, image_norm = unit(placed)
    image_set[0:size, 0:width] = image_unit.astype(BF16)
    image_label = column(image_labels[...].astype(F32))
    image_set[0:size, width:] = jnp.where(lane == 0, image_label, jnp.where(lane == 1, 1.0, 0.0)).astype(BF16)
    image_copies = []
    for at in sorted(range(1, len(reach)), key=lambda at: -abs(reach[at][1])):
        image_copies.append(
            remote(
                block(image_set, 0),
                block(image_set, at),
                image_send.at[at],
                image_recv.at[at],
                blk(reach[at][0], way * reach[at][1], 0),
            )
        )
    for copy in text_copies:
        copy.wait_recv()
    text_copies.append(
        remote(
            text_set.at[pl.ds(0, half), :],
            text_set.at[pl.ds(half, half), :],
            text_send.at[len(text_far)],
            text_recv.at[len(text_far)],
            blk(0, 0, 1),
        )
    )
    text_copies[-1].wait_recv()
    for copy in image_copies:
        copy.wait_recv()

    temp = jnp.exp(jnp.full((1, 1), log_temp[0], F32))
    weights, loss = pairs(image_set[...], text_set[...], width, temp, jnp.full((1, 1), bias[0], F32))
    text_part = dot(weights, image_set[:, :width], TN)
    core_back[...] = text_part[half:].astype(BF16)
    core_copy = remote(core_back, core_got, core_send.at[0], core_recv.at[0], blk(0, 0, 1))
    image_part = dot(weights, text_set[:, :width])

    def tails(data):
        wide_lane = iota((data.shape[0], LANES), 1)
        high, low = split(data, 2)
        return jnp.where(
            wide_lane == 0, high.astype(F32), jnp.where(wide_lane == 1, low.astype(F32), 0.0)
        ).astype(BF16)

    def tail(data):
        return jnp.sum(data.astype(F32), axis=1, keepdims=True)

    side_back[:, 0:width] = image_part[near * size :].astype(BF16)
    side_back[:, width:] = tails(loss[near * size :])
    order = sorted(range(near), key=lambda at: -abs(image_far[at]))
    side_copies = {}
    for at in order:
        side_copies[at] = remote(
            block(side_back, at), block(side_got, at), side_send.at[at], side_recv.at[at], blk(1, 0, 0)
        )
    core_copy.wait_recv()
    text_sum = text_part[:half] + core_got[...].astype(F32)
    text_back[...] = text_sum.astype(BF16)
    back_copies = {}
    for at in range(len(text_far)):
        back_copies[at] = remote(
            block(text_back, at),
            block(text_got, at),
            tback_send.at[at],
            tback_recv.at[at],
            blk(0, -text_far[at], 0),
        )
    iback_copies = {}
    for at in order:
        side_copies[at].wait_recv()
        rows = slice(at * size, (at + 1) * size)
        image_sum = image_part[rows] + side_got[rows, 0:width].astype(F32)
        loss_sum = loss[rows] + tail(side_got[rows, width:])
        if image_far[at]:
            image_back[rows, 0:width] = image_sum.astype(BF16)
            image_back[rows, width:] = tails(loss_sum)
            iback_copies[at] = remote(
                block(image_back, at),
                block(image_got, at),
                iback_send.at[at],
                iback_recv.at[at],
                blk(0, -way * image_far[at], 0),
            )
    for at, copy in iback_copies.items():
        copy.wait_recv()
        rows = slice(at * size, (at + 1) * size)
        image_sum = image_sum + image_got[rows, :width].astype(F32)
        loss_sum = loss_sum + tail(image_got[rows, width:])
    image_out[...] = back(image_sum, image_unit, image_norm).astype(BF16)
    loss_sum = loss_sum / F32(len(reach) * len(text_far) * 2 * size)
    same = iota((size, size), 0) == iota((size, size), 1)
    loss_out[...] = jnp.sum(jnp.where(same, jnp.broadcast_to(loss_sum, (size, size)), 0.0), axis=0, keepdims=True)
    text_unit, text_norm = kept["text"]
    total = jnp.zeros((size, width), F32)
    for at, copy in back_copies.items():
        copy.wait_recv()
        total = total + text_got[at * size : (at + 1) * size, :].astype(F32)
    text_out[...] = back(total, text_unit, text_norm).astype(BF16)

    last = [core_copy] + list(side_copies.values()) + list(iback_copies.values()) + list(back_copies.values())
    for copy in row_copies + text_copies + image_copies + last:
        copy.wait_send()


def solution(mesh):
    depth = mesh.shape["blk"] // 4
    peers = mesh.shape["group"]
    image_far, text_far = offsets(depth)
    near = len(image_far)
    lines = len(text_far)

    def body(
        patches,
        patch_counts,
        dest_list,
        probe,
        w_attn_out,
        w_key,
        w_value,
        texts,
        image_labels,
        text_labels,
        log_temp,
        bias,
    ):
        rows, width = patches.shape
        size = texts.shape[0]
        padded = -(-rows // LANES) * LANES
        far = pl.BlockSpec(memory_space=pl.ANY)
        local = pl.BlockSpec(memory_space=pltpu.VMEM)
        dma = lambda n: pltpu.SemaphoreType.DMA((n,))
        image_grad, text_grad, row_loss = pl.pallas_call(
            functools.partial(kernel, depth, peers),
            out_shape=(
                pltpu.VMEM((size, width), BF16),
                pltpu.VMEM((size, width), BF16),
                pltpu.VMEM((1, size), F32),
            ),
            in_specs=[far] * 10 + [pl.BlockSpec(memory_space=pltpu.SMEM)] * 2,
            out_specs=(local, local, local),
            scratch_shapes=[
                pltpu.VMEM((1, peers), jnp.int32),
                pltpu.VMEM((1, peers), jnp.int32),
                pltpu.VMEM((width,), BF16),
                pltpu.VMEM((1, size), jnp.int32),
                pltpu.VMEM((1, size), jnp.int32),
                pltpu.VMEM((rows, width), BF16),
                pltpu.VMEM((width, width), BF16),
                pltpu.VMEM((width, width), BF16),
                pltpu.VMEM((width, width), BF16),
                pltpu.VMEM((size, width), BF16),
                pltpu.VMEM((padded, width), F32),
                pltpu.VMEM((peers, 1, width), F32),
                pltpu.VMEM((peers, 1, width), F32),
                pltpu.VMEM((size, width + LANES), BF16),
                pltpu.VMEM((2 * lines * size, width + LANES), BF16),
                pltpu.VMEM((2 * near * size, width + LANES), BF16),
                pltpu.VMEM((near * size, width + LANES), BF16),
                pltpu.VMEM((near * size, width + LANES), BF16),
                pltpu.VMEM((near * size, width + LANES), BF16),
                pltpu.VMEM((near * size, width + LANES), BF16),
                pltpu.VMEM((lines * size, width), BF16),
                pltpu.VMEM((lines * size, width), BF16),
                pltpu.VMEM((lines * size, width), BF16),
                pltpu.VMEM((lines * size, width), BF16),
                dma(7 + 3 * parts(width)),
                dma(peers),
                dma(peers),
                dma(lines + 1),
                dma(lines + 1),
                dma(2 * near),
                dma(2 * near),
                dma(near),
                dma(near),
                dma(lines),
                dma(lines),
                dma(1),
                dma(1),
                dma(near),
                dma(near),
            ],
            compiler_params=pltpu.CompilerParams(
                collective_id=0, has_side_effects=True, vmem_limit_bytes=62 * 1024 * 1024
            ),
            cost_estimate=pl.CostEstimate(
                flops=8 * rows * width * width, bytes_accessed=8 * width * width, transcendentals=0
            ),
            name="pool_and_contrast",
        )(
            patches,
            patch_counts,
            dest_list,
            probe,
            w_attn_out,
            w_key,
            w_value,
            texts,
            image_labels.reshape(1, size),
            text_labels.reshape(1, size),
            log_temp,
            bias,
        )
        return (image_grad, text_grad, row_loss.reshape(size))

    whole = P(("blk", "group"), None)
    flat = P(("blk", "group"))
    return jax.shard_map(
        body,
        mesh=mesh,
        in_specs=(whole, whole, whole, P(), P(), P(), P(), whole, flat, flat, P(), P()),
        out_specs=(whole, whole, flat),
        check_vma=False,
    )
```

profile of v0, /device:TPU:1, one launch (start us, length us, event | category | flops | bytes accessed | tf_op | source)
XLA Modules:
  0.0 55.6 jit_solution(7391462847896286196)
XLA Ops:
  1.9 51.9 %pool_and_contrast.1 = (bf16[16,1152]{1,0:T(8,128)(2,1)S(1)}, bf16[16,1152]{1,0:T(8,128)(2,1)S(1)}, f32[1,16]{1,0:T(1,128)S(1)}) custom-call(bf16[376,1152]{1,0:T(8,128)(2,1)} %patches.1, s32[1,16]{1,0:T(1,128)} %counts_hbm.1, s32[1,16]{1,0:T(1,128)} %dest_hbm.1, bf16[1152]{0:T(1024)(128)(2,1)} %probe_hbm.1, bf16[1152,1152]{1,0:T(8,128)(2,1)} %w_proj.1, ...), custom_call_target="tpu_custom_call" | custom-call | flops 3991928832 | bytes 10616832 | tf_op jit(solution)/shard_map/pool_and_contrast/pallas_call | solution.py:438
  53.8 0.6 %copy.18 = bf16[16,1152]{1,0:T(8,128)(2,1)} copy(bf16[16,1152]{1,0:T(8,128)(2,1)S(1)} %get-tuple-element.9) | data formatting | bytes 73728
  54.4 0.5 copy.20
  54.9 0.6 %copy.19 = bf16[16,1152]{1,0:T(8,128)(2,1)} copy(bf16[16,1152]{1,0:T(8,128)(2,1)S(1)} %get-tuple-element.10) | data formatting | bytes 73728
where the time goes:
time: 55.7 us; the launch traced here: 55.6 us
  Pallas kernels  51.9 us (93%)
  between operations  1.94 us (3%)
  local copies, waits for them, and re-layouts  1.75 us (3%)
    pallas_call x1, Pallas kernels, body(): pl.pallas_call(functools.partial(kernel, depth, peers), out_shape=(pltpu....  51.9 us
    unnamed x3, local copies, waits for them, and re-layouts  1.75 us

commit v1 on v0

--- a/solution.py
+++ b/solution.py
@@ -276,11 +276,22 @@
             text_own[:, 0:width] = text_unit.astype(BF16)
             text_label = column(text_labels[...].astype(F32))
             text_own[:, width:] = jnp.where(lane == 0, 1.0, jnp.where(lane == 1, -text_label, 0.0)).astype(BF16)
+        if name == "value" and cut == 0:
+            pl.semaphore_wait(barrier, len(known) + peers - 1)
+            for at in range(len(text_far)):
+                text_copies.append(
+                    remote(
+                        text_own,
+                        block(text_set, at),
+                        text_send.at[at],
+                        text_recv.at[at],
+                        blk(0, text_far[at], 0),
+                    )
+                )
 
     ordered = pool(patch_buf, counts, dest, probe, key_buf, proj_buf, value_buf, ready, normed)
     for at in range(peers):
         row_out[at] = ordered[at : at + 1, :]
-    pl.semaphore_wait(barrier, len(known) + peers - 1)
     row_copies = []
     for step in sorted(range(1, peers), key=lambda step: abs(step - peers // 2)):
         to = (mine + step) % peers
@@ -290,17 +301,6 @@
             )
         )
     row_in[mine] = row_out[mine]
-    for at in range(len(text_far)):
-        text_copies.append(
-            remote(
-                text_own,
-                block(text_set, at),
-                text_send.at[at],
-                text_recv.at[at],
-                blk(0, text_far[at], 0),
-            )
-        )
-
     for copy in row_copies:
         copy.wait_recv()
     placed = jnp.concatenate([row_in[at] for at in range(peers)], axis=0)
@@ -338,7 +338,10 @@
     weights, loss = pairs(image_set[...], text_set[...], width, temp, jnp.full((1, 1), bias[0], F32))
     text_part = dot(weights, image_set[:, :width], TN)
     core_back[...] = text_part[half:].astype(BF16)
-    core_copy = remote(core_back, core_got, core_send.at[0], core_recv.at[0], blk(0, 0, 1))
+    core_copies = [
+        remote(block(core_back, at), block(core_got, at), core_send.at[at], core_recv.at[at], blk(0, 0, 1))
+        for at in range(len(text_far))
+    ]
     image_part = dot(weights, text_set[:, :width])
 
     def tails(data):
@@ -359,11 +362,11 @@
         side_copies[at] = remote(
             block(side_back, at), block(side_got, at), side_send.at[at], side_recv.at[at], blk(1, 0, 0)
         )
-    core_copy.wait_recv()
-    text_sum = text_part[:half] + core_got[...].astype(F32)
-    text_back[...] = text_sum.astype(BF16)
     back_copies = {}
     for at in range(len(text_far)):
+        core_copies[at].wait_recv()
+        rows = slice(at * size, (at + 1) * size)
+        text_back[rows, :] = (text_part[rows] + core_got[rows, :].astype(F32)).astype(BF16)
         back_copies[at] = remote(
             block(text_back, at),
             block(text_got, at),
@@ -403,7 +406,7 @@
         total = total + text_got[at * size : (at + 1) * size, :].astype(F32)
     text_out[...] = back(total, text_unit, text_norm).astype(BF16)
 
-    last = [core_copy] + list(side_copies.values()) + list(iback_copies.values()) + list(back_copies.values())
+    last = core_copies + list(side_copies.values()) + list(iback_copies.values()) + list(back_copies.values())
     for copy in row_copies + text_copies + image_copies + last:
         copy.wait_send()
 
@@ -480,8 +483,8 @@
                 dma(near),
                 dma(lines),
                 dma(lines),
-                dma(1),
-                dma(1),
+                dma(lines),
+                dma(lines),
                 dma(near),
                 dma(near),
             ],

time: 55.7 us -> 55.7 us (level)
  no operation moved by 1% of the time
where the time goes in v1:
time: 55.7 us; the launch traced here: 55.6 us
  Pallas kernels  51.9 us (93%)
  between operations  1.94 us (3%)
  local copies, waits for them, and re-layouts  1.75 us (3%)
    pallas_call x1, Pallas kernels, body(): pl.pallas_call(functools.partial(kernel, depth, peers), out_shape=(pltpu....  51.9 us
    unnamed x3, local copies, waits for them, and re-layouts  1.75 us

profile of v1, /device:TPU:1, one launch (start us, length us, event | category | flops | bytes accessed | tf_op | source)
XLA Modules:
  0.0 55.6 jit_solution(11444386657995840355)
XLA Ops:
  1.9 51.9 %pool_and_contrast.1 = (bf16[16,1152]{1,0:T(8,128)(2,1)S(1)}, bf16[16,1152]{1,0:T(8,128)(2,1)S(1)}, f32[1,16]{1,0:T(1,128)S(1)}) custom-call(bf16[376,1152]{1,0:T(8,128)(2,1)} %patches.1, s32[1,16]{1,0:T(1,128)} %counts_hbm.1, s32[1,16]{1,0:T(1,128)} %dest_hbm.1, bf16[1152]{0:T(1024)(128)(2,1)} %probe_hbm.1, bf16[1152,1152]{1,0:T(8,128)(2,1)} %w_proj.1, ...), custom_call_target="tpu_custom_call" | custom-call | flops 3991928832 | bytes 10616832 | tf_op jit(solution)/shard_map/pool_and_contrast/pallas_call | solution.py:441
  53.8 0.6 %copy.18 = bf16[16,1152]{1,0:T(8,128)(2,1)} copy(bf16[16,1152]{1,0:T(8,128)(2,1)S(1)} %get-tuple-element.9) | data formatting | bytes 73728
  54.4 0.5 copy.20
  54.9 0.6 %copy.19 = bf16[16,1152]{1,0:T(8,128)(2,1)} copy(bf16[16,1152]{1,0:T(8,128)(2,1)S(1)} %get-tuple-element.10) | data formatting | bytes 73728

commit v2 on v1

--- a/solution.py
+++ b/solution.py
@@ -301,13 +301,14 @@
             )
         )
     row_in[mine] = row_out[mine]
+    image_label = column(image_labels[...].astype(F32))
+    image_set[0:size, width:] = jnp.where(lane == 0, image_label, jnp.where(lane == 1, 1.0, 0.0)).astype(BF16)
+    temp = jnp.exp(jnp.full((1, 1), log_temp[0], F32))
     for copy in row_copies:
         copy.wait_recv()
     placed = jnp.concatenate([row_in[at] for at in range(peers)], axis=0)
     image_unit, image_norm = unit(placed)
     image_set[0:size, 0:width] = image_unit.astype(BF16)
-    image_label = column(image_labels[...].astype(F32))
-    image_set[0:size, width:] = jnp.where(lane == 0, image_label, jnp.where(lane == 1, 1.0, 0.0)).astype(BF16)
     image_copies = []
     for at in sorted(range(1, len(reach)), key=lambda at: -abs(reach[at][1])):
         image_copies.append(
@@ -334,15 +335,12 @@
     for copy in image_copies:
         copy.wait_recv()
 
-    temp = jnp.exp(jnp.full((1, 1), log_temp[0], F32))
     weights, loss = pairs(image_set[...], text_set[...], width, temp, jnp.full((1, 1), bias[0], F32))
-    text_part = dot(weights, image_set[:, :width], TN)
-    core_back[...] = text_part[half:].astype(BF16)
+    core_back[...] = dot(weights[:, half:], image_set[:, :width], TN).astype(BF16)
     core_copies = [
         remote(block(core_back, at), block(core_got, at), core_send.at[at], core_recv.at[at], blk(0, 0, 1))
         for at in range(len(text_far))
     ]
-    image_part = dot(weights, text_set[:, :width])
 
     def tails(data):
         wide_lane = iota((data.shape[0], LANES), 1)
@@ -354,7 +352,7 @@
     def tail(data):
         return jnp.sum(data.astype(F32), axis=1, keepdims=True)
 
-    side_back[:, 0:width] = image_part[near * size :].astype(BF16)
+    side_back[:, 0:width] = dot(weights[near * size :], text_set[:, :width]).astype(BF16)
     side_back[:, width:] = tails(loss[near * size :])
     order = sorted(range(near), key=lambda at: -abs(image_far[at]))
     side_copies = {}
@@ -362,6 +360,8 @@
         side_copies[at] = remote(
             block(side_back, at), block(side_got, at), side_send.at[at], side_recv.at[at], blk(1, 0, 0)
         )
+    text_part = dot(weights[:, :half], image_set[:, :width], TN)
+    image_part = dot(weights[: near * size], text_set[:, :width])
     back_copies = {}
     for at in range(len(text_far)):
         core_copies[at].wait_recv()

time: 55.7 us -> 55.9 us (level)
  no operation moved by 1% of the time
where the time goes in v2:
time: 55.9 us; the launch traced here: 55.8 us
  Pallas kernels  52.1 us (93%)
  between operations  1.94 us (3%)
  local copies, waits for them, and re-layouts  1.75 us (3%)
    pallas_call x1, Pallas kernels, body(): pl.pallas_call(functools.partial(kernel, depth, peers), out_shape=(pltpu....  52.1 us
    unnamed x3, local copies, waits for them, and re-layouts  1.75 us

profile of v2, /device:TPU:1, one launch (start us, length us, event | category | flops | bytes accessed | tf_op | source)
XLA Modules:
  0.0 55.8 jit_solution(6057364908282072871)
XLA Ops:
  1.9 52.1 %pool_and_contrast.1 = (bf16[16,1152]{1,0:T(8,128)(2,1)S(1)}, bf16[16,1152]{1,0:T(8,128)(2,1)S(1)}, f32[1,16]{1,0:T(1,128)S(1)}) custom-call(bf16[376,1152]{1,0:T(8,128)(2,1)} %patches.1, s32[1,16]{1,0:T(1,128)} %counts_hbm.1, s32[1,16]{1,0:T(1,128)} %dest_hbm.1, bf16[1152]{0:T(1024)(128)(2,1)} %probe_hbm.1, bf16[1152,1152]{1,0:T(8,128)(2,1)} %w_proj.1, ...), custom_call_target="tpu_custom_call" | custom-call | flops 3991928832 | bytes 10616832 | tf_op jit(solution)/shard_map/pool_and_contrast/pallas_call | solution.py:441
  54.0 0.6 %copy.18 = bf16[16,1152]{1,0:T(8,128)(2,1)} copy(bf16[16,1152]{1,0:T(8,128)(2,1)S(1)} %get-tuple-element.9) | data formatting | bytes 73728
  54.6 0.5 copy.20
  55.1 0.6 %copy.19 = bf16[16,1152]{1,0:T(8,128)(2,1)} copy(bf16[16,1152]{1,0:T(8,128)(2,1)S(1)} %get-tuple-element.10) | data formatting | bytes 73728

commit v3 on v2

--- a/solution.py
+++ b/solution.py
@@ -358,7 +358,11 @@
     side_copies = {}
     for at in order:
         side_copies[at] = remote(
-            block(side_back, at), block(side_got, at), side_send.at[at], side_recv.at[at], blk(1, 0, 0)
+            block(side_back, at),
+            block(side_got, at),
+            side_send.at[at],
+            side_recv.at[at],
+            blk(1, -way * image_far[at], 0),
         )
     text_part = dot(weights[:, :half], image_set[:, :width], TN)
     image_part = dot(weights[: near * size], text_set[:, :width])
@@ -374,15 +378,11 @@
             tback_recv.at[at],
             blk(0, -text_far[at], 0),
         )
+    image_back[:, 0:width] = image_part.astype(BF16)
+    image_back[:, width:] = tails(loss[: near * size])
     iback_copies = {}
     for at in order:
-        side_copies[at].wait_recv()
-        rows = slice(at * size, (at + 1) * size)
-        image_sum = image_part[rows] + side_got[rows, 0:width].astype(F32)
-        loss_sum = loss[rows] + tail(side_got[rows, width:])
         if image_far[at]:
-            image_back[rows, 0:width] = image_sum.astype(BF16)
-            image_back[rows, width:] = tails(loss_sum)
             iback_copies[at] = remote(
                 block(image_back, at),
                 block(image_got, at),
@@ -390,11 +390,14 @@
                 iback_recv.at[at],
                 blk(0, -way * image_far[at], 0),
             )
-    for at, copy in iback_copies.items():
-        copy.wait_recv()
-        rows = slice(at * size, (at + 1) * size)
-        image_sum = image_sum + image_got[rows, :width].astype(F32)
-        loss_sum = loss_sum + tail(image_got[rows, width:])
+    image_sum = image_part[:size]
+    loss_sum = loss[:size]
+    for got, copies in ((side_got, side_copies), (image_got, iback_copies)):
+        for at, copy in copies.items():
+            copy.wait_recv()
+            rows = slice(at * size, (at + 1) * size)
+            image_sum = image_sum + got[rows, :width].astype(F32)
+            loss_sum = loss_sum + tail(got[rows, width:])
     image_out[...] = back(image_sum, image_unit, image_norm).astype(BF16)
     loss_sum = loss_sum / F32(len(reach) * len(text_far) * 2 * size)
     same = iota((size, size), 0) == iota((size, size), 1)

time: 55.9 us -> 56.4 us (level)
  no operation moved by 1% of the time
where the time goes in v3:
time: 56.4 us; the launch traced here: 56.3 us
  Pallas kernels  52.6 us (93%)
  between operations  1.94 us (3%)
  local copies, waits for them, and re-layouts  1.75 us (3%)
    pallas_call x1, Pallas kernels, body(): pl.pallas_call(functools.partial(kernel, depth, peers), out_shape=(pltpu....  52.6 us
    unnamed x3, local copies, waits for them, and re-layouts  1.75 us

profile of v3, /device:TPU:1, one launch (start us, length us, event | category | flops | bytes accessed | tf_op | source)
XLA Modules:
  0.0 56.3 jit_solution(3863899961217423731)
XLA Ops:
  1.9 52.6 %pool_and_contrast.1 = (bf16[16,1152]{1,0:T(8,128)(2,1)S(1)}, bf16[16,1152]{1,0:T(8,128)(2,1)S(1)}, f32[1,16]{1,0:T(1,128)S(1)}) custom-call(bf16[376,1152]{1,0:T(8,128)(2,1)} %patches.1, s32[1,16]{1,0:T(1,128)} %counts_hbm.1, s32[1,16]{1,0:T(1,128)} %dest_hbm.1, bf16[1152]{0:T(1024)(128)(2,1)} %probe_hbm.1, bf16[1152,1152]{1,0:T(8,128)(2,1)} %w_proj.1, ...), custom_call_target="tpu_custom_call" | custom-call | flops 3991928832 | bytes 10616832 | tf_op jit(solution)/shard_map/pool_and_contrast/pallas_call | solution.py:444
  54.5 0.6 %copy.18 = bf16[16,1152]{1,0:T(8,128)(2,1)} copy(bf16[16,1152]{1,0:T(8,128)(2,1)S(1)} %get-tuple-element.9) | data formatting | bytes 73728
  55.1 0.5 copy.20
  55.6 0.6 %copy.19 = bf16[16,1152]{1,0:T(8,128)(2,1)} copy(bf16[16,1152]{1,0:T(8,128)(2,1)S(1)} %get-tuple-element.10) | data formatting | bytes 73728
